TPU v7x, 32 devices: a whole 2x2x4 slice. The times are simulated.
32 devices in a mesh: tiles: 2 (over x), date: 8 (over z, y), row: 2 (over core).
Axes of the slice: x: 2, y: 2, z: 4, core: 2. Of those that a mesh axis runs over, the one named last changes fastest.
Arguments:
- slc_stack: bfloat16 [16, 2, 256, 1024], P('date', None, ('tiles', 'row')), parts along dimension 2, as said below
- partners: int32 [16, 4], P('date'), may hold values from 0 to 15, as said below
- counts: int32 [16], P('date'), may hold values from 1 to 4, as said below
- windows: int32 [16, 4], P('date'), may hold values from 3 to 5
Outputs:
- coherence: bfloat16 [16, 4, 256, 1024], P('date', None, ('tiles', 'row')), parts along dimension 2
There are 2 independent parts, one for each index of `tiles`. A program takes and returns all parts, laid end to end along the dimension named above; an argument that names none is the same for every part. Nothing has to cross between parts.
Inputs may be any that keep to these rules, and one draw needn't show every extreme that they name: The partners of date d are (d + o) mod 16 for distinct offsets o from 1 to 4; some date has a first partner exactly 4 ahead. `counts`: of the 2 dates held by one device along `date`, at most one has more than 2 pairs, so those dates have 6 pairs or fewer together; some device's pair of dates has exactly 6, and some date has 4. `slc_stack`: every pixel's magnitude is 0.5 or more.
All inputs are finite; a program needn't handle non-finite values.
Results may differ from a plain program's by a relative error of at most 0.001.
Values may be sent and summed in bfloat16 or wider, within the bound.
A program may use at most 64 MiB of HBM per device.

v0:
```python
import jax
import jax.numpy as jnp
from jax import lax
from jax.sharding import PartitionSpec as P


def extended_2(shard, sides, width):
    for axis, dim in sides:
        count, length = (lax.axis_size(axis), shard.shape[dim])
        up = [(i, (i + 1) % count) for i in range(count - 1)]
        down = [(j, i) for i, j in up]
        last = lax.slice_in_dim(shard, length - width, length, axis=dim)
        leading = lax.slice_in_dim(shard, 0, width, axis=dim)
        before = lax.ppermute(last, axis, up)
        after = lax.ppermute(leading, axis, down)
        shard = jnp.concatenate([before, shard, after], axis=dim)
    return shard


def from_behind(shard, axis, by):
    count = lax.axis_size(axis)
    return lax.ppermute(shard, axis, [(i, (i + by) % count) for i in range(count)])


def pair_products(first_block, second_block):
    first_re = first_block[0].astype(jnp.float32)
    first_im = first_block[1].astype(jnp.float32)
    second_re = second_block[0].astype(jnp.float32)
    second_im = second_block[1].astype(jnp.float32)
    cross_re = first_re * second_re + first_im * second_im
    cross_im = first_im * second_re - first_re * second_im
    power_first = first_re * first_re + first_im * first_im
    power_second = second_re * second_re + second_im * second_im
    return jnp.stack([cross_re, cross_im, power_first, power_second])


def range_boxcar(stacked, half_width):
    columns = stacked.shape[-1]
    padded = jnp.pad(stacked, ((0, 0), (0, 0), (5, 5)))
    summed = jnp.zeros_like(stacked)
    for offset in range(-5, 6):
        weight = jnp.where(half_width >= abs(offset), 1.0, 0.0).astype(jnp.float32)
        summed = summed + weight * padded[:, :, 5 + offset : 5 + offset + columns]
    return summed


def row_boxcar(extended, strip_rows):
    summed = extended[:, 0:strip_rows, :]
    for offset in range(1, 5):
        summed = summed + extended[:, offset : offset + strip_rows, :]
    return summed


def coherence_of(sums):
    magnitude = jnp.sqrt(sums[0] * sums[0] + sums[1] * sums[1])
    return magnitude / jnp.sqrt(sums[2] * sums[3])


def pair_value(window, own_index, partner_date, half_width, first_date, total_dates, strip_rows):
    local_index = jnp.mod(partner_date - first_date, total_dates)
    first_block = lax.dynamic_index_in_dim(window, own_index, 0, keepdims=False)
    second_block = lax.dynamic_index_in_dim(window, local_index, 0, keepdims=False)
    summed = range_boxcar(pair_products(first_block, second_block), half_width)
    summed = extended_2(summed, (("row", 1),), 2)
    return coherence_of(row_boxcar(summed, strip_rows))


def run_items(
    window,
    first_date,
    total_dates,
    strip_rows,
    own_index,
    flat_partners,
    flat_widths,
    needed,
    capacity,
):
    item_total = own_index.shape[0]

    def compute(state_in, slot_item):
        index_own, partner_date, half_width, used_flag = slot_item
        result = pair_value(
            window, index_own, partner_date, half_width, first_date, total_dates, strip_rows
        )
        return (state_in, jnp.where(used_flag, result, 0.0).astype(jnp.bfloat16))

    item_ids = jnp.arange(item_total, dtype=jnp.int32)
    ranking = jnp.where(needed, 0, 1).astype(jnp.int32) * item_total + item_ids
    ordering = jnp.argsort(ranking, stable=True)[0:capacity]
    unused_state, values = lax.scan(
        compute,
        jnp.int32(0),
        (own_index[ordering], flat_partners[ordering], flat_widths[ordering], needed[ordering]),
    )
    blocks = jnp.zeros((item_total,) + values.shape[1:], jnp.bfloat16).at[ordering].set(values)
    return blocks


def local(slc_stack, partners, counts, windows):
    dates_dev = slc_stack.shape[0]
    strip_rows = slc_stack.shape[2]
    per_date = partners.shape[1]
    slot_total = dates_dev * per_date
    loop_size = lax.axis_size("date")
    reach_blocks = loop_size // 4
    total_dates = dates_dev * loop_size
    first_date = lax.axis_index("date") * dates_dev
    half_count = per_date // 2
    capacity = dates_dev * half_count + per_date - half_count
    slot_ids = jnp.arange(slot_total, dtype=jnp.int32)
    local_dates = slot_ids // per_date
    flat_partners = partners.reshape(slot_total)
    flat_widths = windows.reshape(slot_total)
    is_used = slot_ids % per_date < jnp.repeat(counts, per_date)
    pieces = [slc_stack]
    current = slc_stack
    for distance in range(reach_blocks):
        current = from_behind(current, "date", -1)
        pieces.append(current)
    window = jnp.concatenate(pieces, axis=0)
    blocks = run_items(
        window,
        first_date,
        total_dates,
        strip_rows,
        local_dates,
        flat_partners,
        flat_widths,
        is_used,
        capacity,
    )
    return blocks.reshape(dates_dev, per_date, strip_rows, slc_stack.shape[3])


def solution(mesh):
    in_specs = (
        P("date", None, ("tiles", "row"), None),
        P("date", None),
        P("date"),
        P("date", None),
    )
    out_specs = P("date", None, ("tiles", "row"), None)
    return jax.shard_map(local, mesh=mesh, in_specs=in_specs, out_specs=out_specs, check_vma=False)
```

profile of v0, /device:TPU:28, one launch (start us, length us, event | category | flops | bytes accessed | tf_op | source)
XLA Modules:
  0.0 148.0 jit_solution(11523229353198327064)
XLA Ops:
  0.5 0.7 broadcast_in_dim.29
  1.3 15.3 %collective-permute-done.2 = bf16[2,2,64,1024]{3,2,1,0:T(8,128)(2,1)S(1)} collective-permute-done((bf16[2,2,64,1024]{3,2,1,0:T(8,128)(2,1)}, bf16[2,2,64,1024]{3,2,1,0:T(8,128)(2,1)S(1)}, u32[]{:S(2)}, u32[]{:S(2)}) %collective-permute-start.2) | collective-permute-done | bytes 524320 | tf_op jit(solution)/shard_map/ppermute | solution.py:22
  16.6 0.8 reshape.211
  17.4 1.0 sort.17
  19.0 0.6 gather_fusion.1
  19.6 0.6 gather_fusion.2
  20.4 1.2 gather_fusion.3
  21.6 10.6 %collective-permute-done.3 = bf16[2,2,64,1024]{3,2,1,0:T(8,128)(2,1)} collective-permute-done((bf16[2,2,64,1024]{3,2,1,0:T(8,128)(2,1)S(1)}, bf16[2,2,64,1024]{3,2,1,0:T(8,128)(2,1)}, u32[]{:S(2)}, u32[]{:S(2)}) %collective-permute-start.3) | collective-permute-done | bytes 524320 | tf_op jit(solution)/shard_map/ppermute | solution.py:22
  32.2 1.2 pad_maximum_fusion.3
  33.4 112.7 %while.12 = (s32[]{:T(128)}, bf16[6,64,1024]{2,1,0:T(8,128)(2,1)S(1)}, pred[6]{0:T(512)(128)(4,1)S(1)}, s32[6]{0:T(128)S(1)}, s32[6]{0:T(128)S(1)}, /*index=5*/b...) while((s32[]{:T(128)}, ...), condition=%wide.region_2.3_spmd, body=%wide.region_1.2_spmd.sunk | while | flops 9895969 | bytes 9503421 | solution.py:91
  33.4 1.3 dynamic_slice.43
  37.2 0.7 dynamic_slice.45
  43.0 2.8 %fusion.50 = f32[4,64,1024]{2,1,0:T(8,128)S(1)} fusion(f32[4,64,1024]{2,1,0:T(8,128)S(1)} %pad_maximum_fusion.5, f32[]{:T(128)} %bitcast.31, f32[]{:T(128)} %bitcast.32, f32[]{:T(128)} %bitcast.33, f32[]{:T(128)} %bitcast.34, f32[]{:T(128)} %bitcast.35, f32[]{:T(128)} %bitcast.36), kind=kLoop, calls=%fused_computation.29.clone.1 | loop fusion | flops 5505024 | bytes 2097176 | tf_op jit(solution)/shard_map/while/body/eval_jaxpr/add | solution.py:43
  45.8 1.3 collective-permute-start
  47.1 3.0 %collective-permute-start.1 = (f32[4,2,1024]{2,1,0:T(2,128)S(1)}, f32[4,2,1024]{2,1,0:T(2,128)S(1)}, u32[]{:S(2)}, u32[]{:S(2)}) collective-permute-start(f32[4,2,1024]{2,1,0:T(2,128)S(1)} %get-tuple-element.195), channel_id=1, source_target_pairs={{0,1},{2,3},{4,5},{6,7},{8,9},{10,11},{12,13},{14,15},{16,17},{18,... | collective-permute-start | bytes 98312 | tf_op jit(solution)/shard_map/while/body/eval_jaxpr/ppermute | solution.py:14
  51.4 0.8 fusion.53
  52.2 1.3 dynamic_slice.43
  56.0 0.7 dynamic_slice.45
  61.7 2.8 %fusion.50 = f32[4,64,1024]{2,1,0:T(8,128)S(1)} fusion(f32[4,64,1024]{2,1,0:T(8,128)S(1)} %pad_maximum_fusion.5, f32[]{:T(128)} %bitcast.31, f32[]{:T(128)} %bitcast.32, f32[]{:T(128)} %bitcast.33, f32[]{:T(128)} %bitcast.34, f32[]{:T(128)} %bitcast.35, f32[]{:T(128)} %bitcast.36), kind=kLoop, calls=%fused_computation.29.clone.1 | loop fusion | flops 5505024 | bytes 2097176 | tf_op jit(solution)/shard_map/while/body/eval_jaxpr/add | solution.py:43
  64.6 1.3 collective-permute-start
  65.9 3.0 %collective-permute-start.1 = (f32[4,2,1024]{2,1,0:T(2,128)S(1)}, f32[4,2,1024]{2,1,0:T(2,128)S(1)}, u32[]{:S(2)}, u32[]{:S(2)}) collective-permute-start(f32[4,2,1024]{2,1,0:T(2,128)S(1)} %get-tuple-element.195), channel_id=1, source_target_pairs={{0,1},{2,3},{4,5},{6,7},{8,9},{10,11},{12,13},{14,15},{16,17},{18,... | collective-permute-start | bytes 98312 | tf_op jit(solution)/shard_map/while/body/eval_jaxpr/ppermute | solution.py:14
  70.2 0.8 fusion.53
  71.0 1.3 dynamic_slice.43
  74.8 0.7 dynamic_slice.45
  80.5 2.8 %fusion.50 = f32[4,64,1024]{2,1,0:T(8,128)S(1)} fusion(f32[4,64,1024]{2,1,0:T(8,128)S(1)} %pad_maximum_fusion.5, f32[]{:T(128)} %bitcast.31, f32[]{:T(128)} %bitcast.32, f32[]{:T(128)} %bitcast.33, f32[]{:T(128)} %bitcast.34, f32[]{:T(128)} %bitcast.35, f32[]{:T(128)} %bitcast.36), kind=kLoop, calls=%fused_computation.29.clone.1 | loop fusion | flops 5505024 | bytes 2097176 | tf_op jit(solution)/shard_map/while/body/eval_jaxpr/add | solution.py:43
  83.3 1.3 collective-permute-start
  84.6 3.0 %collective-permute-start.1 = (f32[4,2,1024]{2,1,0:T(2,128)S(1)}, f32[4,2,1024]{2,1,0:T(2,128)S(1)}, u32[]{:S(2)}, u32[]{:S(2)}) collective-permute-start(f32[4,2,1024]{2,1,0:T(2,128)S(1)} %get-tuple-element.195), channel_id=1, source_target_pairs={{0,1},{2,3},{4,5},{6,7},{8,9},{10,11},{12,13},{14,15},{16,17},{18,... | collective-permute-start | bytes 98312 | tf_op jit(solution)/shard_map/while/body/eval_jaxpr/ppermute | solution.py:14
  89.0 0.8 fusion.53
  89.8 1.3 dynamic_slice.43
  93.6 0.7 dynamic_slice.45
  99.3 2.8 %fusion.50 = f32[4,64,1024]{2,1,0:T(8,128)S(1)} fusion(f32[4,64,1024]{2,1,0:T(8,128)S(1)} %pad_maximum_fusion.5, f32[]{:T(128)} %bitcast.31, f32[]{:T(128)} %bitcast.32, f32[]{:T(128)} %bitcast.33, f32[]{:T(128)} %bitcast.34, f32[]{:T(128)} %bitcast.35, f32[]{:T(128)} %bitcast.36), kind=kLoop, calls=%fused_computation.29.clone.1 | loop fusion | flops 5505024 | bytes 2097176 | tf_op jit(solution)/shard_map/while/body/eval_jaxpr/add | solution.py:43
  102.1 1.3 collective-permute-start
  103.4 3.0 %collective-permute-start.1 = (f32[4,2,1024]{2,1,0:T(2,128)S(1)}, f32[4,2,1024]{2,1,0:T(2,128)S(1)}, u32[]{:S(2)}, u32[]{:S(2)}) collective-permute-start(f32[4,2,1024]{2,1,0:T(2,128)S(1)} %get-tuple-element.195), channel_id=1, source_target_pairs={{0,1},{2,3},{4,5},{6,7},{8,9},{10,11},{12,13},{14,15},{16,17},{18,... | collective-permute-start | bytes 98312 | tf_op jit(solution)/shard_map/while/body/eval_jaxpr/ppermute | solution.py:14
  107.8 0.8 fusion.53
  108.6 1.3 dynamic_slice.43
  112.4 0.7 dynamic_slice.45
  118.1 2.8 %fusion.50 = f32[4,64,1024]{2,1,0:T(8,128)S(1)} fusion(f32[4,64,1024]{2,1,0:T(8,128)S(1)} %pad_maximum_fusion.5, f32[]{:T(128)} %bitcast.31, f32[]{:T(128)} %bitcast.32, f32[]{:T(128)} %bitcast.33, f32[]{:T(128)} %bitcast.34, f32[]{:T(128)} %bitcast.35, f32[]{:T(128)} %bitcast.36), kind=kLoop, calls=%fused_computation.29.clone.1 | loop fusion | flops 5505024 | bytes 2097176 | tf_op jit(solution)/shard_map/while/body/eval_jaxpr/add | solution.py:43
  120.9 1.3 collective-permute-start
  122.2 3.0 %collective-permute-start.1 = (f32[4,2,1024]{2,1,0:T(2,128)S(1)}, f32[4,2,1024]{2,1,0:T(2,128)S(1)}, u32[]{:S(2)}, u32[]{:S(2)}) collective-permute-start(f32[4,2,1024]{2,1,0:T(2,128)S(1)} %get-tuple-element.195), channel_id=1, source_target_pairs={{0,1},{2,3},{4,5},{6,7},{8,9},{10,11},{12,13},{14,15},{16,17},{18,... | collective-permute-start | bytes 98312 | tf_op jit(solution)/shard_map/while/body/eval_jaxpr/ppermute | solution.py:14
  126.6 0.8 fusion.53
  127.3 1.3 dynamic_slice.43
  131.2 0.7 dynamic_slice.45
  136.9 2.8 %fusion.50 = f32[4,64,1024]{2,1,0:T(8,128)S(1)} fusion(f32[4,64,1024]{2,1,0:T(8,128)S(1)} %pad_maximum_fusion.5, f32[]{:T(128)} %bitcast.31, f32[]{:T(128)} %bitcast.32, f32[]{:T(128)} %bitcast.33, f32[]{:T(128)} %bitcast.34, f32[]{:T(128)} %bitcast.35, f32[]{:T(128)} %bitcast.36), kind=kLoop, calls=%fused_computation.29.clone.1 | loop fusion | flops 5505024 | bytes 2097176 | tf_op jit(solution)/shard_map/while/body/eval_jaxpr/add | solution.py:43
  139.7 1.3 collective-permute-start
  141.0 3.0 %collective-permute-start.1 = (f32[4,2,1024]{2,1,0:T(2,128)S(1)}, f32[4,2,1024]{2,1,0:T(2,128)S(1)}, u32[]{:S(2)}, u32[]{:S(2)}) collective-permute-start(f32[4,2,1024]{2,1,0:T(2,128)S(1)} %get-tuple-element.195), channel_id=1, source_target_pairs={{0,1},{2,3},{4,5},{6,7},{8,9},{10,11},{12,13},{14,15},{16,17},{18,... | collective-permute-start | bytes 98312 | tf_op jit(solution)/shard_map/while/body/eval_jaxpr/ppermute | solution.py:14
  145.3 0.8 fusion.53
  146.3 0.8 scatter_fusion
  147.1 1.0 copy-done
  (65 shorter events, 14.4 us)
Async XLA Ops:
  0.0 32.2 %copy-start.1 = (bf16[2,2,64,1024]{3,2,1,0:T(8,128)(2,1)S(1)}, bf16[2,2,64,1024]{3,2,1,0:T(8,128)(2,1)}, u32[]{:S(2)}) copy-start(bf16[2,2,64,1024]{3,2,1,0:T(8,128)(2,1)} %param.6) | copy-start | bytes 1572868
  0.0 20.3 %copy-start.2 = (s32[2,4]{1,0:T(2,128)S(1)}, s32[2,4]{1,0:T(2,128)}, u32[]{:S(2)}) copy-start(s32[2,4]{1,0:T(2,128)} %param.7) | copy-start | bytes 100
  0.0 16.6 %collective-permute-start.2 = (bf16[2,2,64,1024]{3,2,1,0:T(8,128)(2,1)}, bf16[2,2,64,1024]{3,2,1,0:T(8,128)(2,1)S(1)}, u32[]{:S(2)}, u32[]{:S(2)}) collective-permute-start(bf16[2,2,64,1024]{3,2,1,0:T(8,128)(2,1)} %param.6), channel_id=1, source_target_pairs={{0,14},{2,0},{4,2},{6,4},{8,6},{10,8},{12,10},{14,12},{1,15},{3,1}... | collective-permute-start | bytes 1572872 | tf_op jit(solution)/shard_map/ppermute | solution.py:22
  16.6 15.6 %collective-permute-start.3 = (bf16[2,2,64,1024]{3,2,1,0:T(8,128)(2,1)S(1)}, bf16[2,2,64,1024]{3,2,1,0:T(8,128)(2,1)}, u32[]{:S(2)}, u32[]{:S(2)}) collective-permute-start(bf16[2,2,64,1024]{3,2,1,0:T(8,128)(2,1)S(1)} %collective-permute-done.2), channel_id=1, source_target_pairs={{0,14},{2,0},{4,2},{6,4},{8,6},{10,8},{12,10},{14,12},{1,15},{3,1}... | collective-permute-start | bytes 1572872 | tf_op jit(solution)/shard_map/ppermute | solution.py:22
  45.8 5.0 %collective-permute-start = (f32[4,2,1024]{2,1,0:T(2,128)S(1)}, f32[4,2,1024]{2,1,0:T(2,128)S(1)}, u32[]{:S(2)}, u32[]{:S(2)}) collective-permute-start(f32[4,2,1024]{2,1,0:T(2,128)S(1)} %get-tuple-element.194), channel_id=1, source_target_pairs={{1,0},{3,2},{5,4},{7,6},{9,8},{11,10},{13,12},{15,14},{17,16},{19,... | collective-permute-start | bytes 98312 | tf_op jit(solution)/shard_map/while/body/eval_jaxpr/ppermute | solution.py:15
  47.1 3.9 %collective-permute-start.1 = (f32[4,2,1024]{2,1,0:T(2,128)S(1)}, f32[4,2,1024]{2,1,0:T(2,128)S(1)}, u32[]{:S(2)}, u32[]{:S(2)}) collective-permute-start(f32[4,2,1024]{2,1,0:T(2,128)S(1)} %get-tuple-element.195), channel_id=1, source_target_pairs={{0,1},{2,3},{4,5},{6,7},{8,9},{10,11},{12,13},{14,15},{16,17},{18,... | collective-permute-start | bytes 98312 | tf_op jit(solution)/shard_map/while/body/eval_jaxpr/ppermute | solution.py:14
  64.6 5.0 %collective-permute-start = (f32[4,2,1024]{2,1,0:T(2,128)S(1)}, f32[4,2,1024]{2,1,0:T(2,128)S(1)}, u32[]{:S(2)}, u32[]{:S(2)}) collective-permute-start(f32[4,2,1024]{2,1,0:T(2,128)S(1)} %get-tuple-element.194), channel_id=1, source_target_pairs={{1,0},{3,2},{5,4},{7,6},{9,8},{11,10},{13,12},{15,14},{17,16},{19,... | collective-permute-start | bytes 98312 | tf_op jit(solution)/shard_map/while/body/eval_jaxpr/ppermute | solution.py:15
  65.9 3.9 %collective-permute-start.1 = (f32[4,2,1024]{2,1,0:T(2,128)S(1)}, f32[4,2,1024]{2,1,0:T(2,128)S(1)}, u32[]{:S(2)}, u32[]{:S(2)}) collective-permute-start(f32[4,2,1024]{2,1,0:T(2,128)S(1)} %get-tuple-element.195), channel_id=1, source_target_pairs={{0,1},{2,3},{4,5},{6,7},{8,9},{10,11},{12,13},{14,15},{16,17},{18,... | collective-permute-start | bytes 98312 | tf_op jit(solution)/shard_map/while/body/eval_jaxpr/ppermute | solution.py:14
  83.3 5.0 %collective-permute-start = (f32[4,2,1024]{2,1,0:T(2,128)S(1)}, f32[4,2,1024]{2,1,0:T(2,128)S(1)}, u32[]{:S(2)}, u32[]{:S(2)}) collective-permute-start(f32[4,2,1024]{2,1,0:T(2,128)S(1)} %get-tuple-element.194), channel_id=1, source_target_pairs={{1,0},{3,2},{5,4},{7,6},{9,8},{11,10},{13,12},{15,14},{17,16},{19,... | collective-permute-start | bytes 98312 | tf_op jit(solution)/shard_map/while/body/eval_jaxpr/ppermute | solution.py:15
  84.6 3.9 %collective-permute-start.1 = (f32[4,2,1024]{2,1,0:T(2,128)S(1)}, f32[4,2,1024]{2,1,0:T(2,128)S(1)}, u32[]{:S(2)}, u32[]{:S(2)}) collective-permute-start(f32[4,2,1024]{2,1,0:T(2,128)S(1)} %get-tuple-element.195), channel_id=1, source_target_pairs={{0,1},{2,3},{4,5},{6,7},{8,9},{10,11},{12,13},{14,15},{16,17},{18,... | collective-permute-start | bytes 98312 | tf_op jit(solution)/shard_map/while/body/eval_jaxpr/ppermute | solution.py:14
  102.1 5.0 %collective-permute-start = (f32[4,2,1024]{2,1,0:T(2,128)S(1)}, f32[4,2,1024]{2,1,0:T(2,128)S(1)}, u32[]{:S(2)}, u32[]{:S(2)}) collective-permute-start(f32[4,2,1024]{2,1,0:T(2,128)S(1)} %get-tuple-element.194), channel_id=1, source_target_pairs={{1,0},{3,2},{5,4},{7,6},{9,8},{11,10},{13,12},{15,14},{17,16},{19,... | collective-permute-start | bytes 98312 | tf_op jit(solution)/shard_map/while/body/eval_jaxpr/ppermute | solution.py:15
  103.4 3.9 %collective-permute-start.1 = (f32[4,2,1024]{2,1,0:T(2,128)S(1)}, f32[4,2,1024]{2,1,0:T(2,128)S(1)}, u32[]{:S(2)}, u32[]{:S(2)}) collective-permute-start(f32[4,2,1024]{2,1,0:T(2,128)S(1)} %get-tuple-element.195), channel_id=1, source_target_pairs={{0,1},{2,3},{4,5},{6,7},{8,9},{10,11},{12,13},{14,15},{16,17},{18,... | collective-permute-start | bytes 98312 | tf_op jit(solution)/shard_map/while/body/eval_jaxpr/ppermute | solution.py:14
  120.9 5.0 %collective-permute-start = (f32[4,2,1024]{2,1,0:T(2,128)S(1)}, f32[4,2,1024]{2,1,0:T(2,128)S(1)}, u32[]{:S(2)}, u32[]{:S(2)}) collective-permute-start(f32[4,2,1024]{2,1,0:T(2,128)S(1)} %get-tuple-element.194), channel_id=1, source_target_pairs={{1,0},{3,2},{5,4},{7,6},{9,8},{11,10},{13,12},{15,14},{17,16},{19,... | collective-permute-start | bytes 98312 | tf_op jit(solution)/shard_map/while/body/eval_jaxpr/ppermute | solution.py:15
  122.2 3.9 %collective-permute-start.1 = (f32[4,2,1024]{2,1,0:T(2,128)S(1)}, f32[4,2,1024]{2,1,0:T(2,128)S(1)}, u32[]{:S(2)}, u32[]{:S(2)}) collective-permute-start(f32[4,2,1024]{2,1,0:T(2,128)S(1)} %get-tuple-element.195), channel_id=1, source_target_pairs={{0,1},{2,3},{4,5},{6,7},{8,9},{10,11},{12,13},{14,15},{16,17},{18,... | collective-permute-start | bytes 98312 | tf_op jit(solution)/shard_map/while/body/eval_jaxpr/ppermute | solution.py:14
  139.7 5.0 %collective-permute-start = (f32[4,2,1024]{2,1,0:T(2,128)S(1)}, f32[4,2,1024]{2,1,0:T(2,128)S(1)}, u32[]{:S(2)}, u32[]{:S(2)}) collective-permute-start(f32[4,2,1024]{2,1,0:T(2,128)S(1)} %get-tuple-element.194), channel_id=1, source_target_pairs={{1,0},{3,2},{5,4},{7,6},{9,8},{11,10},{13,12},{15,14},{17,16},{19,... | collective-permute-start | bytes 98312 | tf_op jit(solution)/shard_map/while/body/eval_jaxpr/ppermute | solution.py:15
  141.0 3.9 %collective-permute-start.1 = (f32[4,2,1024]{2,1,0:T(2,128)S(1)}, f32[4,2,1024]{2,1,0:T(2,128)S(1)}, u32[]{:S(2)}, u32[]{:S(2)}) collective-permute-start(f32[4,2,1024]{2,1,0:T(2,128)S(1)} %get-tuple-element.195), channel_id=1, source_target_pairs={{0,1},{2,3},{4,5},{6,7},{8,9},{10,11},{12,13},{14,15},{16,17},{18,... | collective-permute-start | bytes 98312 | tf_op jit(solution)/shard_map/while/body/eval_jaxpr/ppermute | solution.py:14
  147.1 1.0 copy-start
where the time goes:
time: 150 us; the launch traced here: 148 us
  loops' own time  41.1 us (27%)
  other arithmetic  27.6 us (18%)
  waiting for transfers between devices  27.2 us (18%)
  starting transfers between devices  26.4 us (18%)
  local copies, waits for them, and re-layouts  25.7 us (17%)
    another operation x1, loops' own time, run_items(): lax.scan(compute, jnp.int32(0), (own_index[ordering], flat_partners[order...  41.1 us
    ppermute x2, waiting for transfers between devices, from_behind(): lax.ppermute(shard, axis, [(i, (i + by) % count) for i in range(count)])  25.8 us
    dynamic_slice x24, local copies, waits for them, and re-layouts, run_items(): lax.scan(compute, jnp.int32(0), (own_index[ordering], flat_partners[order...  18.8 us
    ppermute x6, starting transfers between devices, extended_2(): before = lax.ppermute(last, axis, up)  18.2 us
    add x6, other arithmetic, range_boxcar(): summed = summed + weight * padded[:, :, 5 + offset:5 + offset + columns]  16.6 us
    ppermute x6, starting transfers between devices, extended_2(): after = lax.ppermute(leading, axis, down)  7.75 us
    dynamic_update_slice x6, other arithmetic, run_items(): lax.scan(compute, jnp.int32(0), (own_index[ordering], flat_partners[order...  4.6 us
  transfers between devices with their start and end apart: 14, of which 8 were waited for; matrix products, arithmetic and copies ran while one was open for 6% of the time, Pallas kernels for 0%

commit v1 on v0

v1 whole, which is shorter than its diff:
```python
import functools
import jax
import jax.numpy as jnp
from jax import lax
from jax.experimental import pallas as pl
from jax.experimental.pallas import tpu as pltpu
from jax.sharding import PartitionSpec as P

MESH = pl.DeviceIdType.MESH
LANES = 128
PIECE = 32


def exchange_kernel(loop_size, reach, slc_ref, got_ref, edge_ref, pack, *sems):
    direct_send, direct_recv, near_send, near_recv, edge_send, edge_recv = sems
    dates, parts, rows, columns = slc_ref.shape
    tile = lax.axis_index("tiles")
    me = lax.axis_index("date")
    row = lax.axis_index("row")
    pieces = [
        (d, c, pl.ds(r, PIECE)) for d in range(dates) for c in range(parts) for r in range(0, rows, PIECE)
    ]
    relayed = reach == 2

    def at(steps, other=False):
        there = lax.rem(me + steps + loop_size, loop_size)
        return (tile, there, 1 - row if other else row)

    barrier = pltpu.get_barrier_semaphore()

    def greet(device):
        pl.semaphore_signal(barrier, inc=1, device_id=device, device_id_type=MESH)

    even = lax.rem(me, 2) == 0
    for k in range(reach + 1):
        greet(at(k, other=True))
    if relayed:
        greet(at(2))
        greet(at(jnp.where(even, 1, -1)))
    else:
        for k in range(1, reach + 1):
            greet(at(k))

    picked = []
    for d in range(dates):
        for c in range(parts):
            last = slc_ref[d, c, rows - 16 : rows, :].astype(jnp.float32)[14:16]
            first = slc_ref[d, c, 0:16, :].astype(jnp.float32)[0:2]
            picked.append(jnp.where(row == 0, last, first))
    spare = pack.shape[0] - 2 * len(picked)
    if spare:
        picked.append(jnp.zeros((spare, columns), jnp.float32))
    pack[...] = jnp.concatenate(picked, axis=0).astype(jnp.bfloat16)

    pl.semaphore_wait(barrier, 2 * reach + 1)

    def far(k, n):
        d, c, r = pieces[n]
        return pltpu.make_async_remote_copy(
            src_ref=slc_ref.at[d, c, r],
            dst_ref=got_ref.at[k - 1, d, c, r],
            send_sem=direct_send.at[k - 1, n],
            recv_sem=direct_recv.at[k - 1, n],
            device_id=at(-k),
            device_id_type=MESH,
        )

    def near(n, src, steps):
        d, c, r = pieces[n]
        return pltpu.make_async_remote_copy(
            src_ref=src.at[d, c, r],
            dst_ref=got_ref.at[0, d, c, r],
            send_sem=near_send.at[n],
            recv_sem=near_recv.at[n],
            device_id=at(steps),
            device_id_type=MESH,
        )

    def edge(k):
        return pltpu.make_async_remote_copy(
            src_ref=pack,
            dst_ref=edge_ref.at[k],
            send_sem=edge_send.at[k],
            recv_sem=edge_recv.at[k],
            device_id=at(-k, other=True),
            device_id_type=MESH,
        )

    total = range(len(pieces))
    edges = [edge(k) for k in range(reach + 1)]
    if relayed:
        for n in total:
            far(2, n).start()
            if n == 0:
                for e in edges:
                    e.start()

        @pl.when(even)
        def _():
            for n in total:
                far(2, n).wait_recv()
                near(n, got_ref.at[1], 1).start()
            for n in total:
                near(n, got_ref.at[1], 1).wait()

        @pl.when(jnp.logical_not(even))
        def _():
            for n in total:
                near(n, slc_ref, -1).start()
            for n in total:
                far(2, n).wait_recv()
            for n in total:
                near(n, slc_ref, -1).wait()

        for n in total:
            far(2, n).wait_send()
    else:
        for e in edges:
            e.start()
        for n in total:
            for k in range(1, reach + 1):
                far(k, n).start()
        for n in total:
            for k in range(1, reach + 1):
                far(k, n).wait()
    for e in edges:
        e.wait()


def exchange(slc, loop_size, reach):
    dates, parts, rows, columns = slc.shape
    pieces = dates * parts * (rows // PIECE)
    packed = -(-2 * dates * parts // 16) * 16
    return pl.pallas_call(
        functools.partial(exchange_kernel, loop_size, reach),
        out_shape=(
            jax.ShapeDtypeStruct((reach,) + slc.shape, jnp.bfloat16),
            jax.ShapeDtypeStruct((reach + 1, packed, columns), jnp.bfloat16),
        ),
        in_specs=[pl.BlockSpec(memory_space=pltpu.VMEM)],
        out_specs=(pl.BlockSpec(memory_space=pl.ANY), pl.BlockSpec(memory_space=pl.ANY)),
        scratch_shapes=[
            pltpu.VMEM((packed, columns), jnp.bfloat16),
            pltpu.SemaphoreType.DMA((reach, pieces)),
            pltpu.SemaphoreType.DMA((reach, pieces)),
            pltpu.SemaphoreType.DMA((pieces,)),
            pltpu.SemaphoreType.DMA((pieces,)),
            pltpu.SemaphoreType.DMA((reach + 1,)),
            pltpu.SemaphoreType.DMA((reach + 1,)),
        ],
        compiler_params=pltpu.CompilerParams(
            collective_id=0, has_side_effects=True, vmem_limit_bytes=16 << 20
        ),
        name="exchange",
    )(slc)


def shifted(tiles, by, lane):
    rolled = [pltpu.roll(t, by, 1) for t in tiles]
    shifted_tiles = [jnp.where(lane < by, 0.0, rolled[0])]
    for j in range(1, len(tiles)):
        shifted_tiles.append(jnp.where(lane < by, rolled[j - 1], rolled[j]))
    shifted_tiles.append(jnp.where(lane < by, rolled[-1], 0.0))
    return shifted_tiles


def box_columns(tiles, half, lane):
    count = len(tiles)
    zero = jnp.zeros_like(tiles[0])

    def add(x, y):
        x = x + [zero] * (count + 1 - len(x))
        return [a + b for a, b in zip(x, y[: count + 1])]

    two = add(tiles, shifted(tiles, 1, lane))
    three = add(two, shifted(tiles, 2, lane))
    four = add(two, shifted(two, 2, lane))
    seven = add(three, shifted(four, 3, lane))
    rest = [jnp.where(half == 3, 0.0, jnp.where(half == 4, a, b)) for a, b in zip(two, four)]
    return add(seven, shifted(rest, 7, lane))


def coherence_kernel(
    reach, total_dates, meta_ref, partner_ref, count_ref, width_ref, slc_ref, got_ref, edge_ref,
    out_ref, held, edges, ends, products, result, in_sem, out_sem,
):
    dates, parts, rows, columns = slc_ref.shape
    per_date = out_ref.shape[1]
    col_tiles = columns // LANES
    slots = dates * per_date
    first_date = meta_ref[0]
    row = meta_ref[1]
    copies = [
        pltpu.make_async_copy(slc_ref, held.at[pl.ds(0, dates)], in_sem.at[0]),
        pltpu.make_async_copy(edge_ref, edges, in_sem.at[1]),
    ]
    for k in range(reach):
        copies.append(
            pltpu.make_async_copy(got_ref.at[k], held.at[pl.ds((k + 1) * dates, dates)], in_sem.at[2 + k])
        )
    for copy in copies:
        copy.start()
    for copy in copies:
        copy.wait()

    for k in range(reach + 1):
        block = edges[k].astype(jnp.float32)
        for d in range(dates):
            for c in range(parts):
                at = (d * parts + c) * 2
                ends[k * dates + d, c, 0:2, :] = block[at : at + 2]
                ends[k * dates + d, c, 6:8, :] = block[at : at + 2]

    lane = lax.broadcasted_iota(jnp.int32, (16, LANES), 1)

    def write_products(at, count, u_re, u_im, v_re, v_im, keep=None):
        values = (
            u_re * v_re + u_im * v_im,
            u_im * v_re - u_re * v_im,
            u_re * u_re + u_im * u_im,
            v_re * v_re + v_im * v_im,
        )
        for q, value in enumerate(values):
            for j in range(col_tiles):
                part = value[:, j * LANES : (j + 1) * LANES]
                if keep is None:
                    products[q, j, at : at + count, :] = part
                else:
                    products[q, j, 0:8, :] = jnp.where(keep, part, 0.0)
                    products[q, j, rows + 8 : rows + 16, :] = jnp.where(keep, 0.0, part)

    def out_copy(slot):
        d, s = lax.div(slot, per_date), lax.rem(slot, per_date)
        return pltpu.make_async_copy(result.at[slot], out_ref.at[d, s], out_sem.at[slot])

    def one_slot(slot, carry):
        d, s = lax.div(slot, per_date), lax.rem(slot, per_date)
        used = s < count_ref[d]

        @pl.when(used)
        def _():
            v = lax.rem(partner_ref[d, s] - first_date + total_dates, total_dates)
            half = width_ref[d, s]
            write_products(0, 8, ends[d, 0], ends[d, 1], ends[v, 0], ends[v, 1], row == 1)
            for r in range(0, rows, 16):
                write_products(
                    8 + r, 16,
                    *(
                        held[x, c, r : r + 16, :].astype(jnp.float32)
                        for x in (d, v)
                        for c in range(2)
                    ),
                )
            for r in range(0, rows, 16):
                sums = []
                for q in range(4):
                    tiles = []
                    for j in range(col_tiles):
                        taken = [products[q, j, r + 6 + k : r + 22 + k, :] for k in range(5)]
                        tiles.append((taken[0] + taken[1]) + (taken[2] + taken[3]) + taken[4])
                    sums.append(box_columns(tiles, half, lane))
                ratio = [
                    jnp.sqrt(a * a + b * b) * lax.rsqrt(u * w) for a, b, u, w in zip(*sums)
                ]
                back = [pltpu.roll(x, LANES - half, 1) for x in ratio]
                for j in range(col_tiles):
                    value = jnp.where(lane < LANES - half, back[j], back[j + 1])
                    result[slot, r : r + 16, j * LANES : (j + 1) * LANES] = value.astype(jnp.bfloat16)

        @pl.when(jnp.logical_not(used))
        def _():
            result[slot] = jnp.zeros((rows, columns), jnp.bfloat16)

        out_copy(slot).start()
        return carry

    lax.fori_loop(0, slots, one_slot, 0)
    for slot in range(slots):
        out_copy(slot).wait()


def coherence(meta, partners, counts, windows, slc, got, edge, reach, total_dates):
    dates, parts, rows, columns = slc.shape
    per_date = partners.shape[1]
    held = dates * (reach + 1)
    smem = pl.BlockSpec(memory_space=pltpu.SMEM)
    anywhere = pl.BlockSpec(memory_space=pl.ANY)
    return pl.pallas_call(
        functools.partial(coherence_kernel, reach, total_dates),
        out_shape=jax.ShapeDtypeStruct((dates, per_date, rows, columns), jnp.bfloat16),
        in_specs=[smem] * 4 + [anywhere] * 3,
        out_specs=anywhere,
        scratch_shapes=[
            pltpu.VMEM((held, parts, rows, columns), jnp.bfloat16),
            pltpu.VMEM(edge.shape, jnp.bfloat16),
            pltpu.VMEM((held, parts, 8, columns), jnp.float32),
            pltpu.VMEM((4, columns // LANES, rows + 16, LANES), jnp.float32),
            pltpu.VMEM((dates * per_date, rows, columns), jnp.bfloat16),
            pltpu.SemaphoreType.DMA((reach + 2,)),
            pltpu.SemaphoreType.DMA((dates * per_date,)),
        ],
        compiler_params=pltpu.CompilerParams(vmem_limit_bytes=40 << 20),
        name="coherence",
    )(meta, partners, counts, windows, slc, got, edge)


def local(slc_stack, partners, counts, windows):
    dates = slc_stack.shape[0]
    loop_size = lax.axis_size("date")
    reach = loop_size // 4
    total_dates = dates * loop_size
    meta = jnp.stack([lax.axis_index("date") * dates, lax.axis_index("row")]).astype(jnp.int32)
    got, edge = exchange(slc_stack, loop_size, reach)
    return coherence(meta, partners, counts, windows, slc_stack, got, edge, reach, total_dates)


def solution(mesh):
    in_specs = (
        P("date", None, ("tiles", "row"), None),
        P("date", None),
        P("date"),
        P("date", None),
    )
    out_specs = P("date", None, ("tiles", "row"), None)
    return jax.shard_map(local, mesh=mesh, in_specs=in_specs, out_specs=out_specs, check_vma=False)
```

time: 150 us -> 42.1 us (0.28)
  the two profiles are of different devices: /device:TPU:28 before, /device:TPU:20 now
where the time goes in v1:
time: 42.1 us; the launch traced here: 41.9 us
  Pallas kernels  40.1 us (95%)
  local copies, waits for them, and re-layouts  1.7 us (4%)
    pallas_call x1, Pallas kernels, coherence(): pl.pallas_call(functools.partial(coherence_kernel, reach, total_dates), o...  20.1 us
    pallas_call x1, Pallas kernels, exchange(): pl.pallas_call(functools.partial(exchange_kernel, loop_size, reach), out_...  20 us
    unnamed x10, local copies, waits for them, and re-layouts  1.7 us

profile of v1, /device:TPU:20, one launch (start us, length us, event | category | flops | bytes accessed | tf_op | source)
XLA Modules:
  0.0 41.9 jit_solution(3672857732075536975)
XLA Ops:
  0.0 0.1 pad_add_fusion.meta_ref
  0.1 0.0 copy-start
  0.1 1.0 %copy-done = bf16[2,2,64,1024]{3,2,1,0:T(8,128)(2,1)S(1)} copy-done((bf16[2,2,64,1024]{3,2,1,0:T(8,128)(2,1)S(1)}, bf16[2,2,64,1024]{3,2,1,0:T(8,128)(2,1)}, u32[]{:S(2)}) %copy-start) | copy-done | bytes 524312
  1.1 0.0 copy-start.1
  1.1 0.0 copy-start.3
  1.1 20.0 %exchange.1 = (bf16[2,2,2,64,1024]{4,3,2,1,0:T(8,128)(2,1)S(1)}, bf16[3,16,1024]{2,1,0:T(8,128)(2,1)S(1)}) custom-call(bf16[2,2,64,1024]{3,2,1,0:T(8,128)(2,1)S(1)} %copy-done), custom_call_target="tpu_custom_call" | custom-call | tf_op jit(solution)/shard_map/exchange/pallas_call | solution.py:134
  21.1 0.0 copy-start.2
  21.2 0.0 copy-start.4
  21.2 0.0 copy-done.1
  21.2 0.0 copy-done.3
  21.2 0.6 %copy-done.2 = s32[2,4]{1,0:T(2,128)S(1)} copy-done((s32[2,4]{1,0:T(2,128)S(1)}, s32[2,4]{1,0:T(2,128)}, u32[]{:S(2)}) %copy-start.2) | copy-done | bytes 56
  21.8 0.0 copy-done.4
  21.8 20.1 %coherence.1 = bf16[2,4,64,1024]{3,2,1,0:T(8,128)(2,1)} custom-call(s32[2]{0:T(128)S(1)} %pad_add_fusion.meta_ref, s32[2,4]{1,0:T(2,128)S(1)} %copy-done.2, s32[2]{0:T(128)S(1)} %copy-done.4, s32[2,4]{1,0:T(2,128)S(1)} %copy-done.3, bf16[2,2,64,1024]{3,2,1,0:T(8,128)(2,1)S(1)} %copy-done.1, bf16[2,2,2,64,1024]{4,3,2,1,0:T(8,128)(2,1)S(1)} %get-tuple-element.7.got_ref, ...), custom_call_target="tpu_custom_call" | custom-call | tf_op jit(solution)/shard_map/coherence/pallas_call | solution.py:288
Async XLA Ops:
  0.1 1.0 %copy-start = (bf16[2,2,64,1024]{3,2,1,0:T(8,128)(2,1)S(1)}, bf16[2,2,64,1024]{3,2,1,0:T(8,128)(2,1)}, u32[]{:S(2)}) copy-start(bf16[2,2,64,1024]{3,2,1,0:T(8,128)(2,1)} %slc_ref.3) | copy-start | bytes 1572868
  1.1 20.1 %copy-start.1 = (bf16[2,2,64,1024]{3,2,1,0:T(8,128)(2,1)S(1)}, bf16[2,2,64,1024]{3,2,1,0:T(8,128)(2,1)}, u32[]{:S(2)}) copy-start(bf16[2,2,64,1024]{3,2,1,0:T(8,128)(2,1)} %slc_ref.3) | copy-start | bytes 1572868
  1.1 20.1 %copy-start.3 = (s32[2,4]{1,0:T(2,128)S(1)}, s32[2,4]{1,0:T(2,128)}, u32[]{:S(2)}) copy-start(s32[2,4]{1,0:T(2,128)} %width_ref.1) | copy-start | bytes 100
  21.1 0.7 %copy-start.2 = (s32[2,4]{1,0:T(2,128)S(1)}, s32[2,4]{1,0:T(2,128)}, u32[]{:S(2)}) copy-start(s32[2,4]{1,0:T(2,128)} %partner_ref.1) | copy-start | bytes 100
  21.2 0.7 %copy-start.4 = (s32[2]{0:T(128)S(1)}, s32[2]{0:T(128)}, u32[]{:S(2)}) copy-start(s32[2]{0:T(128)} %count_ref.1) | copy-start | bytes 28

commit v2 on v1

--- a/solution.py
+++ b/solution.py
@@ -9,6 +9,8 @@
 MESH = pl.DeviceIdType.MESH
 LANES = 128
 PIECE = 32
+BLOCK = 256
+HALVES = (3, 4, 5)
 
 
 def exchange_kernel(loop_size, reach, slc_ref, got_ref, edge_ref, pack, *sems):
@@ -155,34 +157,15 @@
     )(slc)
 
 
-def shifted(tiles, by, lane):
-    rolled = [pltpu.roll(t, by, 1) for t in tiles]
-    shifted_tiles = [jnp.where(lane < by, 0.0, rolled[0])]
-    for j in range(1, len(tiles)):
-        shifted_tiles.append(jnp.where(lane < by, rolled[j - 1], rolled[j]))
-    shifted_tiles.append(jnp.where(lane < by, rolled[-1], 0.0))
-    return shifted_tiles
-
-
-def box_columns(tiles, half, lane):
-    count = len(tiles)
-    zero = jnp.zeros_like(tiles[0])
-
-    def add(x, y):
-        x = x + [zero] * (count + 1 - len(x))
-        return [a + b for a, b in zip(x, y[: count + 1])]
-
-    two = add(tiles, shifted(tiles, 1, lane))
-    three = add(two, shifted(tiles, 2, lane))
-    four = add(two, shifted(two, 2, lane))
-    seven = add(three, shifted(four, 3, lane))
-    rest = [jnp.where(half == 3, 0.0, jnp.where(half == 4, a, b)) for a, b in zip(two, four)]
-    return add(seven, shifted(rest, 7, lane))
+def band(half, block):
+    into = lax.broadcasted_iota(jnp.int32, (2 * block, block), 0) - block // 2
+    out = lax.broadcasted_iota(jnp.int32, (2 * block, block), 1)
+    return jnp.where(jnp.abs(into - out) <= half, 1.0, 0.0).astype(jnp.bfloat16)
 
 
 def coherence_kernel(
     reach, total_dates, meta_ref, partner_ref, count_ref, width_ref, slc_ref, got_ref, edge_ref,
-    out_ref, held, edges, ends, products, result, in_sem, out_sem,
+    out_ref, held, edges, ends, products, bands, split, result, in_sem, out_sem,
 ):
     dates, parts, rows, columns = slc_ref.shape
     per_date = out_ref.shape[1]
@@ -200,6 +183,14 @@
         )
     for copy in copies:
         copy.start()
+    for half in HALVES:
+        matrix = band(half, BLOCK)
+        bands[half - HALVES[0], 0 : 2 * BLOCK, :] = matrix
+        bands[half - HALVES[0], 2 * BLOCK : 4 * BLOCK, :] = matrix
+    side = BLOCK // 2
+    zeros = jnp.zeros((2, 4 * rows, side), jnp.bfloat16)
+    split[:, :, 0:side] = zeros
+    split[:, :, side + columns : 2 * side + columns] = zeros
     for copy in copies:
         copy.wait()
 
@@ -210,8 +201,6 @@
                 at = (d * parts + c) * 2
                 ends[k * dates + d, c, 0:2, :] = block[at : at + 2]
                 ends[k * dates + d, c, 6:8, :] = block[at : at + 2]
-
-    lane = lax.broadcasted_iota(jnp.int32, (16, LANES), 1)
 
     def write_products(at, count, u_re, u_im, v_re, v_im, keep=None):
         values = (
@@ -251,21 +240,25 @@
                         for c in range(2)
                     ),
                 )
-            for r in range(0, rows, 16):
-                sums = []
-                for q in range(4):
-                    tiles = []
+            for q in range(4):
+                for r in range(0, rows, 16):
                     for j in range(col_tiles):
                         taken = [products[q, j, r + 6 + k : r + 22 + k, :] for k in range(5)]
-                        tiles.append((taken[0] + taken[1]) + (taken[2] + taken[3]) + taken[4])
-                    sums.append(box_columns(tiles, half, lane))
-                ratio = [
-                    jnp.sqrt(a * a + b * b) * lax.rsqrt(u * w) for a, b, u, w in zip(*sums)
-                ]
-                back = [pltpu.roll(x, LANES - half, 1) for x in ratio]
-                for j in range(col_tiles):
-                    value = jnp.where(lane < LANES - half, back[j], back[j + 1])
-                    result[slot, r : r + 16, j * LANES : (j + 1) * LANES] = value.astype(jnp.bfloat16)
+                        total = (taken[0] + taken[1]) + (taken[2] + taken[3]) + taken[4]
+                        high = total.astype(jnp.bfloat16)
+                        low = (total - high.astype(jnp.float32)).astype(jnp.bfloat16)
+                        at = side + j * LANES
+                        split[0, q * rows + r : q * rows + r + 16, at : at + LANES] = high
+                        split[1, q * rows + r : q * rows + r + 16, at : at + LANES] = low
+            matrix = bands[half - HALVES[0]]
+            for c in range(0, columns, BLOCK):
+                window = jnp.concatenate(
+                    [split[0, :, c : c + 2 * BLOCK], split[1, :, c : c + 2 * BLOCK]], axis=1
+                )
+                box = jnp.dot(window, matrix, preferred_element_type=jnp.float32)
+                box_re, box_im, box_u, box_v = (box[q * rows : (q + 1) * rows] for q in range(4))
+                value = jnp.sqrt(box_re * box_re + box_im * box_im) * lax.rsqrt(box_u * box_v)
+                result[slot, :, c : c + BLOCK] = value.astype(jnp.bfloat16)
 
         @pl.when(jnp.logical_not(used))
         def _():
@@ -295,6 +288,8 @@
             pltpu.VMEM(edge.shape, jnp.bfloat16),
             pltpu.VMEM((held, parts, 8, columns), jnp.float32),
             pltpu.VMEM((4, columns // LANES, rows + 16, LANES), jnp.float32),
+            pltpu.VMEM((len(HALVES), 4 * BLOCK, BLOCK), jnp.bfloat16),
+            pltpu.VMEM((2, 4 * rows, columns + BLOCK), jnp.bfloat16),
             pltpu.VMEM((dates * per_date, rows, columns), jnp.bfloat16),
             pltpu.SemaphoreType.DMA((reach + 2,)),
             pltpu.SemaphoreType.DMA((dates * per_date,)),

time: 42.1 us -> 30.7 us (0.73)
  the two profiles are of different devices: /device:TPU:20 before, /device:TPU:28 now
where the time goes in v2:
time: 30.7 us; the launch traced here: 30.5 us
  Pallas kernels  28.7 us (93%)
  local copies, waits for them, and re-layouts  1.7 us (6%)
    pallas_call x1, Pallas kernels, exchange(): pl.pallas_call(functools.partial(exchange_kernel, loop_size, reach), out_...  21.7 us
    pallas_call x1, Pallas kernels, coherence(): pl.pallas_call(functools.partial(coherence_kernel, reach, total_dates), o...  6.96 us
    unnamed x10, local copies, waits for them, and re-layouts  1.7 us

profile of v2, /device:TPU:28, one launch (start us, length us, event | category | flops | bytes accessed | tf_op | source)
XLA Modules:
  0.0 30.5 jit_solution(6077478360840540436)
XLA Ops:
  0.0 0.1 pad_add_fusion.meta_ref
  0.1 0.0 copy-start
  0.1 1.0 %copy-done = bf16[2,2,64,1024]{3,2,1,0:T(8,128)(2,1)S(1)} copy-done((bf16[2,2,64,1024]{3,2,1,0:T(8,128)(2,1)S(1)}, bf16[2,2,64,1024]{3,2,1,0:T(8,128)(2,1)}, u32[]{:S(2)}) %copy-start) | copy-done | bytes 524312
  1.1 0.0 copy-start.1
  1.1 0.0 copy-start.3
  1.1 21.7 %exchange.1 = (bf16[2,2,2,64,1024]{4,3,2,1,0:T(8,128)(2,1)S(1)}, bf16[3,16,1024]{2,1,0:T(8,128)(2,1)S(1)}) custom-call(bf16[2,2,64,1024]{3,2,1,0:T(8,128)(2,1)S(1)} %copy-done), custom_call_target="tpu_custom_call" | custom-call | tf_op jit(solution)/shard_map/exchange/pallas_call | solution.py:136
  22.9 0.0 copy-start.2
  22.9 0.0 copy-start.4
  22.9 0.0 copy-done.1
  22.9 0.0 copy-done.3
  22.9 0.6 %copy-done.2 = s32[2,4]{1,0:T(2,128)S(1)} copy-done((s32[2,4]{1,0:T(2,128)S(1)}, s32[2,4]{1,0:T(2,128)}, u32[]{:S(2)}) %copy-start.2) | copy-done | bytes 56
  23.6 0.0 copy-done.4
  23.6 7.0 %coherence.1 = bf16[2,4,64,1024]{3,2,1,0:T(8,128)(2,1)} custom-call(s32[2]{0:T(128)S(1)} %pad_add_fusion.meta_ref, s32[2,4]{1,0:T(2,128)S(1)} %copy-done.2, s32[2]{0:T(128)S(1)} %copy-done.4, s32[2,4]{1,0:T(2,128)S(1)} %copy-done.3, bf16[2,2,64,1024]{3,2,1,0:T(8,128)(2,1)S(1)} %copy-done.1, bf16[2,2,2,64,1024]{4,3,2,1,0:T(8,128)(2,1)S(1)} %get-tuple-element.7.got_ref, ...), custom_call_target="tpu_custom_call" | custom-call | tf_op jit(solution)/shard_map/coherence/pallas_call | solution.py:281
Async XLA Ops:
  0.1 1.0 %copy-start = (bf16[2,2,64,1024]{3,2,1,0:T(8,128)(2,1)S(1)}, bf16[2,2,64,1024]{3,2,1,0:T(8,128)(2,1)}, u32[]{:S(2)}) copy-start(bf16[2,2,64,1024]{3,2,1,0:T(8,128)(2,1)} %slc_ref.3) | copy-start | bytes 1572868
  1.1 21.8 %copy-start.1 = (bf16[2,2,64,1024]{3,2,1,0:T(8,128)(2,1)S(1)}, bf16[2,2,64,1024]{3,2,1,0:T(8,128)(2,1)}, u32[]{:S(2)}) copy-start(bf16[2,2,64,1024]{3,2,1,0:T(8,128)(2,1)} %slc_ref.3) | copy-start | bytes 1572868
  1.1 21.8 %copy-start.3 = (s32[2,4]{1,0:T(2,128)S(1)}, s32[2,4]{1,0:T(2,128)}, u32[]{:S(2)}) copy-start(s32[2,4]{1,0:T(2,128)} %width_ref.1) | copy-start | bytes 100
  22.9 0.7 %copy-start.2 = (s32[2,4]{1,0:T(2,128)S(1)}, s32[2,4]{1,0:T(2,128)}, u32[]{:S(2)}) copy-start(s32[2,4]{1,0:T(2,128)} %partner_ref.1) | copy-start | bytes 100
  22.9 0.7 %copy-start.4 = (s32[2]{0:T(128)S(1)}, s32[2]{0:T(128)}, u32[]{:S(2)}) copy-start(s32[2]{0:T(128)} %count_ref.1) | copy-start | bytes 28

commit v3 on v2

--- a/solution.py
+++ b/solution.py
@@ -13,8 +13,8 @@
 HALVES = (3, 4, 5)
 
 
-def exchange_kernel(loop_size, reach, slc_ref, got_ref, edge_ref, pack, *sems):
-    direct_send, direct_recv, near_send, near_recv, edge_send, edge_recv = sems
+def exchange_kernel(loop_size, reach, slc_ref, got_ref, edge_ref, rim, pack, *sems):
+    rim_sem, direct_send, direct_recv, near_send, near_recv, edge_send, edge_recv = sems
     dates, parts, rows, columns = slc_ref.shape
     tile = lax.axis_index("tiles")
     me = lax.axis_index("date")
@@ -43,12 +43,15 @@
         for k in range(1, reach + 1):
             greet(at(k))
 
+    start = pl.multiple_of((1 - row) * (rows - 16), 16)
+    rim_copy = pltpu.make_async_copy(slc_ref.at[:, :, pl.ds(start, 16), :], rim, rim_sem)
+    rim_copy.start()
+    rim_copy.wait()
     picked = []
     for d in range(dates):
         for c in range(parts):
-            last = slc_ref[d, c, rows - 16 : rows, :].astype(jnp.float32)[14:16]
-            first = slc_ref[d, c, 0:16, :].astype(jnp.float32)[0:2]
-            picked.append(jnp.where(row == 0, last, first))
+            near_rows = rim[d, c].astype(jnp.float32)
+            picked.append(jnp.where(row == 0, near_rows[14:16], near_rows[0:2]))
     spare = pack.shape[0] - 2 * len(picked)
     if spare:
         picked.append(jnp.zeros((spare, columns), jnp.float32))
@@ -139,10 +142,12 @@
             jax.ShapeDtypeStruct((reach,) + slc.shape, jnp.bfloat16),
             jax.ShapeDtypeStruct((reach + 1, packed, columns), jnp.bfloat16),
         ),
-        in_specs=[pl.BlockSpec(memory_space=pltpu.VMEM)],
+        in_specs=[pl.BlockSpec(memory_space=pl.ANY)],
         out_specs=(pl.BlockSpec(memory_space=pl.ANY), pl.BlockSpec(memory_space=pl.ANY)),
         scratch_shapes=[
+            pltpu.VMEM((dates, parts, 16, columns), jnp.bfloat16),
             pltpu.VMEM((packed, columns), jnp.bfloat16),
+            pltpu.SemaphoreType.DMA,
             pltpu.SemaphoreType.DMA((reach, pieces)),
             pltpu.SemaphoreType.DMA((reach, pieces)),
             pltpu.SemaphoreType.DMA((pieces,)),
@@ -164,15 +169,16 @@
 
 
 def coherence_kernel(
-    reach, total_dates, meta_ref, partner_ref, count_ref, width_ref, slc_ref, got_ref, edge_ref,
-    out_ref, held, edges, ends, products, bands, split, result, in_sem, out_sem,
+    reach, total_dates, partner_hbm, count_hbm, width_hbm, slc_ref, got_ref, edge_ref,
+    out_ref, held, edges, ends, products, bands, split, result,
+    partner_ref, count_ref, width_ref, in_sem, out_sem,
 ):
     dates, parts, rows, columns = slc_ref.shape
     per_date = out_ref.shape[1]
     col_tiles = columns // LANES
     slots = dates * per_date
-    first_date = meta_ref[0]
-    row = meta_ref[1]
+    first_date = lax.axis_index("date") * dates
+    row = lax.axis_index("row")
     copies = [
         pltpu.make_async_copy(slc_ref, held.at[pl.ds(0, dates)], in_sem.at[0]),
         pltpu.make_async_copy(edge_ref, edges, in_sem.at[1]),
@@ -181,6 +187,9 @@
         copies.append(
             pltpu.make_async_copy(got_ref.at[k], held.at[pl.ds((k + 1) * dates, dates)], in_sem.at[2 + k])
         )
+    scalars = ((partner_hbm, partner_ref), (count_hbm, count_ref), (width_hbm, width_ref))
+    for n, (src, dst) in enumerate(scalars):
+        copies.append(pltpu.make_async_copy(src, dst, in_sem.at[2 + reach + n]))
     for copy in copies:
         copy.start()
     for half in HALVES:
@@ -272,16 +281,15 @@
         out_copy(slot).wait()
 
 
-def coherence(meta, partners, counts, windows, slc, got, edge, reach, total_dates):
+def coherence(partners, counts, windows, slc, got, edge, reach, total_dates):
     dates, parts, rows, columns = slc.shape
     per_date = partners.shape[1]
     held = dates * (reach + 1)
-    smem = pl.BlockSpec(memory_space=pltpu.SMEM)
     anywhere = pl.BlockSpec(memory_space=pl.ANY)
     return pl.pallas_call(
         functools.partial(coherence_kernel, reach, total_dates),
         out_shape=jax.ShapeDtypeStruct((dates, per_date, rows, columns), jnp.bfloat16),
-        in_specs=[smem] * 4 + [anywhere] * 3,
+        in_specs=[anywhere] * 6,
         out_specs=anywhere,
         scratch_shapes=[
             pltpu.VMEM((held, parts, rows, columns), jnp.bfloat16),
@@ -291,12 +299,15 @@
             pltpu.VMEM((len(HALVES), 4 * BLOCK, BLOCK), jnp.bfloat16),
             pltpu.VMEM((2, 4 * rows, columns + BLOCK), jnp.bfloat16),
             pltpu.VMEM((dates * per_date, rows, columns), jnp.bfloat16),
-            pltpu.SemaphoreType.DMA((reach + 2,)),
+            pltpu.SMEM(partners.shape, jnp.int32),
+            pltpu.SMEM(counts.shape, jnp.int32),
+            pltpu.SMEM(windows.shape, jnp.int32),
+            pltpu.SemaphoreType.DMA((reach + 5,)),
             pltpu.SemaphoreType.DMA((dates * per_date,)),
         ],
         compiler_params=pltpu.CompilerParams(vmem_limit_bytes=40 << 20),
         name="coherence",
-    )(meta, partners, counts, windows, slc, got, edge)
+    )(partners, counts, windows, slc, got, edge)
 
 
 def local(slc_stack, partners, counts, windows):
@@ -304,9 +315,8 @@
     loop_size = lax.axis_size("date")
     reach = loop_size // 4
     total_dates = dates * loop_size
-    meta = jnp.stack([lax.axis_index("date") * dates, lax.axis_index("row")]).astype(jnp.int32)
     got, edge = exchange(slc_stack, loop_size, reach)
-    return coherence(meta, partners, counts, windows, slc_stack, got, edge, reach, total_dates)
+    return coherence(partners, counts, windows, slc_stack, got, edge, reach, total_dates)
 
 
 def solution(mesh):

time: 30.7 us -> 31.5 us (1.026)
  Pallas kernels: 28.7 us -> 29.6 us
    pallas_call x1, Pallas kernels: 6.96 us -> 7.81 us  [coherence(): pl.pallas_call(functools.partial(coherence_kernel, reach, total_dates), o...]
where the time goes in v3:
time: 31.5 us; the launch traced here: 31.3 us
  Pallas kernels  29.6 us (94%)
  local copies, waits for them, and re-layouts  1.7 us (5%)
    pallas_call x1, Pallas kernels, exchange(): pl.pallas_call(functools.partial(exchange_kernel, loop_size, reach), out_...  21.8 us
    pallas_call x1, Pallas kernels, coherence(): pl.pallas_call(functools.partial(coherence_kernel, reach, total_dates), o...  7.81 us
    unnamed x10, local copies, waits for them, and re-layouts  1.7 us

profile of v3, /device:TPU:28, one launch (start us, length us, event | category | flops | bytes accessed | tf_op | source)
XLA Modules:
  0.0 31.3 jit_solution(826471389865423623)
XLA Ops:
  0.0 0.0 copy-start
  0.0 1.0 %copy-done = bf16[2,2,64,1024]{3,2,1,0:T(8,128)(2,1)S(1)} copy-done((bf16[2,2,64,1024]{3,2,1,0:T(8,128)(2,1)S(1)}, bf16[2,2,64,1024]{3,2,1,0:T(8,128)(2,1)}, u32[]{:S(2)}) %copy-start) | copy-done | bytes 524312
  1.0 0.0 copy-start.1
  1.0 0.0 copy-start.3
  1.0 21.8 %exchange.1 = (bf16[2,2,2,64,1024]{4,3,2,1,0:T(8,128)(2,1)S(1)}, bf16[3,16,1024]{2,1,0:T(8,128)(2,1)S(1)}) custom-call(bf16[2,2,64,1024]{3,2,1,0:T(8,128)(2,1)S(1)} %copy-done), custom_call_target="tpu_custom_call" | custom-call | tf_op jit(solution)/shard_map/exchange/pallas_call | solution.py:139
  22.8 0.0 copy-start.2
  22.8 0.0 copy-start.4
  22.8 0.0 copy-done.1
  22.8 0.0 copy-done.3
  22.9 0.6 %copy-done.2 = s32[2,4]{1,0:T(2,128)S(1)} copy-done((s32[2,4]{1,0:T(2,128)S(1)}, s32[2,4]{1,0:T(2,128)}, u32[]{:S(2)}) %copy-start.2) | copy-done | bytes 56
  23.5 0.0 copy-done.4
  23.5 7.8 %coherence.1 = bf16[2,4,64,1024]{3,2,1,0:T(8,128)(2,1)} custom-call(s32[2,4]{1,0:T(2,128)S(1)} %copy-done.2, s32[2]{0:T(128)S(1)} %copy-done.4, s32[2,4]{1,0:T(2,128)S(1)} %copy-done.3, bf16[2,2,64,1024]{3,2,1,0:T(8,128)(2,1)S(1)} %copy-done.1, bf16[2,2,2,64,1024]{4,3,2,1,0:T(8,128)(2,1)S(1)} %get-tuple-element.7.got_ref, ...), custom_call_target="tpu_custom_call" | custom-call | tf_op jit(solution)/shard_map/coherence/pallas_call | solution.py:289
Async XLA Ops:
  0.0 1.0 %copy-start = (bf16[2,2,64,1024]{3,2,1,0:T(8,128)(2,1)S(1)}, bf16[2,2,64,1024]{3,2,1,0:T(8,128)(2,1)}, u32[]{:S(2)}) copy-start(bf16[2,2,64,1024]{3,2,1,0:T(8,128)(2,1)} %slc_ref.3) | copy-start | bytes 1572868
  1.0 21.8 %copy-start.1 = (bf16[2,2,64,1024]{3,2,1,0:T(8,128)(2,1)S(1)}, bf16[2,2,64,1024]{3,2,1,0:T(8,128)(2,1)}, u32[]{:S(2)}) copy-start(bf16[2,2,64,1024]{3,2,1,0:T(8,128)(2,1)} %slc_ref.3) | copy-start | bytes 1572868
  1.0 21.8 %copy-start.3 = (s32[2,4]{1,0:T(2,128)S(1)}, s32[2,4]{1,0:T(2,128)}, u32[]{:S(2)}) copy-start(s32[2,4]{1,0:T(2,128)} %width_hbm.1) | copy-start | bytes 100
  22.8 0.7 %copy-start.2 = (s32[2,4]{1,0:T(2,128)S(1)}, s32[2,4]{1,0:T(2,128)}, u32[]{:S(2)}) copy-start(s32[2,4]{1,0:T(2,128)} %partner_hbm.1) | copy-start | bytes 100
  22.8 0.7 %copy-start.4 = (s32[2]{0:T(128)S(1)}, s32[2]{0:T(128)}, u32[]{:S(2)}) copy-start(s32[2]{0:T(128)} %count_hbm.1) | copy-start | bytes 28

commit v4 on v3

--- a/solution.py
+++ b/solution.py
@@ -14,7 +14,7 @@
 
 
 def exchange_kernel(loop_size, reach, slc_ref, got_ref, edge_ref, rim, pack, *sems):
-    rim_sem, direct_send, direct_recv, near_send, near_recv, edge_send, edge_recv = sems
+    rim_sem, own_sem, direct_send, direct_recv, near_send, near_recv, edge_send, edge_recv = sems
     dates, parts, rows, columns = slc_ref.shape
     tile = lax.axis_index("tiles")
     me = lax.axis_index("date")
@@ -63,7 +63,7 @@
         d, c, r = pieces[n]
         return pltpu.make_async_remote_copy(
             src_ref=slc_ref.at[d, c, r],
-            dst_ref=got_ref.at[k - 1, d, c, r],
+            dst_ref=got_ref.at[k, d, c, r],
             send_sem=direct_send.at[k - 1, n],
             recv_sem=direct_recv.at[k - 1, n],
             device_id=at(-k),
@@ -74,7 +74,7 @@
         d, c, r = pieces[n]
         return pltpu.make_async_remote_copy(
             src_ref=src.at[d, c, r],
-            dst_ref=got_ref.at[0, d, c, r],
+            dst_ref=got_ref.at[1, d, c, r],
             send_sem=near_send.at[n],
             recv_sem=near_recv.at[n],
             device_id=at(steps),
@@ -93,6 +93,7 @@
 
     total = range(len(pieces))
     edges = [edge(k) for k in range(reach + 1)]
+    own_copy = pltpu.make_async_copy(slc_ref, got_ref.at[0], own_sem)
     if relayed:
         for n in total:
             far(2, n).start()
@@ -100,13 +101,15 @@
                 for e in edges:
                     e.start()
 
+        own_copy.start()
+
         @pl.when(even)
         def _():
             for n in total:
                 far(2, n).wait_recv()
-                near(n, got_ref.at[1], 1).start()
-            for n in total:
-                near(n, got_ref.at[1], 1).wait()
+                near(n, got_ref.at[2], 1).start()
+            for n in total:
+                near(n, got_ref.at[2], 1).wait()
 
         @pl.when(jnp.logical_not(even))
         def _():
@@ -120,6 +123,7 @@
         for n in total:
             far(2, n).wait_send()
     else:
+        own_copy.start()
         for e in edges:
             e.start()
         for n in total:
@@ -130,6 +134,7 @@
                 far(k, n).wait()
     for e in edges:
         e.wait()
+    own_copy.wait()
 
 
 def exchange(slc, loop_size, reach):
@@ -139,14 +144,15 @@
     return pl.pallas_call(
         functools.partial(exchange_kernel, loop_size, reach),
         out_shape=(
-            jax.ShapeDtypeStruct((reach,) + slc.shape, jnp.bfloat16),
+            jax.ShapeDtypeStruct((reach + 1,) + slc.shape, jnp.bfloat16),
             jax.ShapeDtypeStruct((reach + 1, packed, columns), jnp.bfloat16),
         ),
-        in_specs=[pl.BlockSpec(memory_space=pl.ANY)],
+        in_specs=[pl.BlockSpec(memory_space=pltpu.HBM)],
         out_specs=(pl.BlockSpec(memory_space=pl.ANY), pl.BlockSpec(memory_space=pl.ANY)),
         scratch_shapes=[
             pltpu.VMEM((dates, parts, 16, columns), jnp.bfloat16),
             pltpu.VMEM((packed, columns), jnp.bfloat16),
+            pltpu.SemaphoreType.DMA,
             pltpu.SemaphoreType.DMA,
             pltpu.SemaphoreType.DMA((reach, pieces)),
             pltpu.SemaphoreType.DMA((reach, pieces)),
@@ -169,27 +175,20 @@
 
 
 def coherence_kernel(
-    reach, total_dates, partner_hbm, count_hbm, width_hbm, slc_ref, got_ref, edge_ref,
-    out_ref, held, edges, ends, products, bands, split, result,
+    reach, total_dates, partner_hbm, count_hbm, width_hbm, held, edges,
+    out_ref, ends, products, bands, split, result,
     partner_ref, count_ref, width_ref, in_sem, out_sem,
 ):
-    dates, parts, rows, columns = slc_ref.shape
+    blocks, dates, parts, rows, columns = held.shape
     per_date = out_ref.shape[1]
     col_tiles = columns // LANES
     slots = dates * per_date
     first_date = lax.axis_index("date") * dates
     row = lax.axis_index("row")
-    copies = [
-        pltpu.make_async_copy(slc_ref, held.at[pl.ds(0, dates)], in_sem.at[0]),
-        pltpu.make_async_copy(edge_ref, edges, in_sem.at[1]),
-    ]
-    for k in range(reach):
-        copies.append(
-            pltpu.make_async_copy(got_ref.at[k], held.at[pl.ds((k + 1) * dates, dates)], in_sem.at[2 + k])
-        )
+    copies = []
     scalars = ((partner_hbm, partner_ref), (count_hbm, count_ref), (width_hbm, width_ref))
     for n, (src, dst) in enumerate(scalars):
-        copies.append(pltpu.make_async_copy(src, dst, in_sem.at[2 + reach + n]))
+        copies.append(pltpu.make_async_copy(src, dst, in_sem.at[n]))
     for copy in copies:
         copy.start()
     for half in HALVES:
@@ -244,7 +243,7 @@
                 write_products(
                     8 + r, 16,
                     *(
-                        held[x, c, r : r + 16, :].astype(jnp.float32)
+                        held[lax.div(x, dates), lax.rem(x, dates), c, r : r + 16, :].astype(jnp.float32)
                         for x in (d, v)
                         for c in range(2)
                     ),
@@ -281,19 +280,17 @@
         out_copy(slot).wait()
 
 
-def coherence(partners, counts, windows, slc, got, edge, reach, total_dates):
-    dates, parts, rows, columns = slc.shape
+def coherence(partners, counts, windows, got, edge, reach, total_dates):
+    blocks, dates, parts, rows, columns = got.shape
     per_date = partners.shape[1]
     held = dates * (reach + 1)
     anywhere = pl.BlockSpec(memory_space=pl.ANY)
     return pl.pallas_call(
         functools.partial(coherence_kernel, reach, total_dates),
         out_shape=jax.ShapeDtypeStruct((dates, per_date, rows, columns), jnp.bfloat16),
-        in_specs=[anywhere] * 6,
+        in_specs=[pl.BlockSpec(memory_space=pltpu.HBM)] * 3 + [pl.BlockSpec(memory_space=pltpu.VMEM)] * 2,
         out_specs=anywhere,
         scratch_shapes=[
-            pltpu.VMEM((held, parts, rows, columns), jnp.bfloat16),
-            pltpu.VMEM(edge.shape, jnp.bfloat16),
             pltpu.VMEM((held, parts, 8, columns), jnp.float32),
             pltpu.VMEM((4, columns // LANES, rows + 16, LANES), jnp.float32),
             pltpu.VMEM((len(HALVES), 4 * BLOCK, BLOCK), jnp.bfloat16),
@@ -302,12 +299,12 @@
             pltpu.SMEM(partners.shape, jnp.int32),
             pltpu.SMEM(counts.shape, jnp.int32),
             pltpu.SMEM(windows.shape, jnp.int32),
-            pltpu.SemaphoreType.DMA((reach + 5,)),
+            pltpu.SemaphoreType.DMA((3,)),
             pltpu.SemaphoreType.DMA((dates * per_date,)),
         ],
         compiler_params=pltpu.CompilerParams(vmem_limit_bytes=40 << 20),
         name="coherence",
-    )(partners, counts, windows, slc, got, edge)
+    )(partners, counts, windows, got, edge)
 
 
 def local(slc_stack, partners, counts, windows):
@@ -316,7 +313,7 @@
     reach = loop_size // 4
     total_dates = dates * loop_size
     got, edge = exchange(slc_stack, loop_size, reach)
-    return coherence(partners, counts, windows, slc_stack, got, edge, reach, total_dates)
+    return coherence(partners, counts, windows, got, edge, reach, total_dates)
 
 
 def solution(mesh):

time: 31.5 us -> 31.6 us (level)
  local copies, waits for them, and re-layouts: 1.7 us -> 3.05 us
  Pallas kernels: 29.6 us -> 28.3 us
    unnamed x10 -> x8, local copies, waits for them, and re-layouts: 1.7 us -> 3.05 us
    pallas_call x1, Pallas kernels: 7.81 us -> 6.52 us  [coherence(): pl.pallas_call(functools.partial(coherence_kernel, reach, total_dates), o...]
where the time goes in v4:
time: 31.6 us; the launch traced here: 31.3 us
  Pallas kernels  28.3 us (90%)
  local copies, waits for them, and re-layouts  3.05 us (10%)
    pallas_call x1, Pallas kernels, exchange(): pl.pallas_call(functools.partial(exchange_kernel, loop_size, reach), out_...  21.8 us
    pallas_call x1, Pallas kernels, coherence(): pl.pallas_call(functools.partial(coherence_kernel, reach, total_dates), o...  6.52 us
    unnamed x8, local copies, waits for them, and re-layouts  3.05 us

profile of v4, /device:TPU:28, one launch (start us, length us, event | category | flops | bytes accessed | tf_op | source)
XLA Modules:
  0.0 31.3 jit_solution(2613589789691816738)
XLA Ops:
  0.0 0.0 copy-start
  0.0 1.0 %copy-done = bf16[2,2,64,1024]{3,2,1,0:T(8,128)(2,1)S(1)} copy-done((bf16[2,2,64,1024]{3,2,1,0:T(8,128)(2,1)S(1)}, bf16[2,2,64,1024]{3,2,1,0:T(8,128)(2,1)}, u32[]{:S(2)}) %copy-start) | copy-done | bytes 524312
  1.0 21.8 %exchange.1 = (bf16[3,2,2,64,1024]{4,3,2,1,0:T(8,128)(2,1)S(1)}, bf16[3,16,1024]{2,1,0:T(8,128)(2,1)S(1)}) custom-call(bf16[2,2,64,1024]{3,2,1,0:T(8,128)(2,1)S(1)} %copy-done), custom_call_target="tpu_custom_call" | custom-call | tf_op jit(solution)/shard_map/exchange/pallas_call | solution.py:144
  22.8 0.0 copy-start.1
  22.8 0.7 %copy-done.1 = s32[2,4]{1,0:T(2,128)S(1)} copy-done((s32[2,4]{1,0:T(2,128)S(1)}, s32[2,4]{1,0:T(2,128)}, u32[]{:S(2)}) %copy-start.1) | copy-done | bytes 56
  23.5 0.0 copy-start.2
  23.5 0.7 %copy-done.2 = s32[2,4]{1,0:T(2,128)S(1)} copy-done((s32[2,4]{1,0:T(2,128)S(1)}, s32[2,4]{1,0:T(2,128)}, u32[]{:S(2)}) %copy-start.2) | copy-done | bytes 56
  24.2 0.0 copy-start.3
  24.2 0.7 %copy-done.3 = s32[2]{0:T(128)S(1)} copy-done((s32[2]{0:T(128)S(1)}, s32[2]{0:T(128)}, u32[]{:S(2)}) %copy-start.3) | copy-done | bytes 32
  24.8 6.5 %coherence.1 = bf16[2,4,64,1024]{3,2,1,0:T(8,128)(2,1)} custom-call(s32[2,4]{1,0:T(2,128)S(1)} %copy-done.1, s32[2]{0:T(128)S(1)} %copy-done.3, s32[2,4]{1,0:T(2,128)S(1)} %copy-done.2, bf16[3,2,2,64,1024]{4,3,2,1,0:T(8,128)(2,1)S(1)} %get-tuple-element.7.held, bf16[3,16,1024]{2,1,0:T(8,128)(2,1)S(1)} %get-tuple-element.8.edges), custom_call_target="tpu_custom_call" | custom-call | tf_op jit(solution)/shard_map/coherence/pallas_call | solution.py:288
Async XLA Ops:
  0.0 1.0 %copy-start = (bf16[2,2,64,1024]{3,2,1,0:T(8,128)(2,1)S(1)}, bf16[2,2,64,1024]{3,2,1,0:T(8,128)(2,1)}, u32[]{:S(2)}) copy-start(bf16[2,2,64,1024]{3,2,1,0:T(8,128)(2,1)} %slc_ref.1) | copy-start | bytes 1572868
  22.8 0.7 %copy-start.1 = (s32[2,4]{1,0:T(2,128)S(1)}, s32[2,4]{1,0:T(2,128)}, u32[]{:S(2)}) copy-start(s32[2,4]{1,0:T(2,128)} %partner_hbm.1) | copy-start | bytes 100
  23.5 0.7 %copy-start.2 = (s32[2,4]{1,0:T(2,128)S(1)}, s32[2,4]{1,0:T(2,128)}, u32[]{:S(2)}) copy-start(s32[2,4]{1,0:T(2,128)} %width_hbm.1) | copy-start | bytes 100
  24.2 0.7 %copy-start.3 = (s32[2]{0:T(128)S(1)}, s32[2]{0:T(128)}, u32[]{:S(2)}) copy-start(s32[2]{0:T(128)} %count_hbm.1) | copy-start | bytes 28

commit v5 on v4

--- a/solution.py
+++ b/solution.py
@@ -169,15 +169,20 @@
 
 
 def band(half, block):
-    into = lax.broadcasted_iota(jnp.int32, (2 * block, block), 0) - block // 2
-    out = lax.broadcasted_iota(jnp.int32, (2 * block, block), 1)
-    return jnp.where(jnp.abs(into - out) <= half, 1.0, 0.0).astype(jnp.bfloat16)
+    def weights(into, out):
+        return jnp.where(jnp.abs(into - out) <= half, 1.0, 0.0).astype(jnp.bfloat16)
+
+    into = lax.broadcasted_iota(jnp.int32, (block, block), 0)
+    out = lax.broadcasted_iota(jnp.int32, (block, block), 1)
+    lane = into[:LANES]
+    beside = jnp.where(lane < LANES // 2, block + lane, lane - LANES)
+    return weights(into, out), weights(beside, out[:LANES])
 
 
 def coherence_kernel(
-    reach, total_dates, partner_hbm, count_hbm, width_hbm, held, edges,
+    reach, total_dates, partner_ref, count_ref, width_ref, held, edges,
     out_ref, ends, products, bands, split, result,
-    partner_ref, count_ref, width_ref, in_sem, out_sem,
+    out_sem,
 ):
     blocks, dates, parts, rows, columns = held.shape
     per_date = out_ref.shape[1]
@@ -185,22 +190,15 @@
     slots = dates * per_date
     first_date = lax.axis_index("date") * dates
     row = lax.axis_index("row")
-    copies = []
-    scalars = ((partner_hbm, partner_ref), (count_hbm, count_ref), (width_hbm, width_ref))
-    for n, (src, dst) in enumerate(scalars):
-        copies.append(pltpu.make_async_copy(src, dst, in_sem.at[n]))
-    for copy in copies:
-        copy.start()
     for half in HALVES:
-        matrix = band(half, BLOCK)
-        bands[half - HALVES[0], 0 : 2 * BLOCK, :] = matrix
-        bands[half - HALVES[0], 2 * BLOCK : 4 * BLOCK, :] = matrix
+        middle, outer = band(half, BLOCK)
+        for n, part in enumerate((middle, middle, outer, outer)):
+            at = (n * BLOCK) if n < 2 else (2 * BLOCK + (n - 2) * LANES)
+            bands[half - HALVES[0], at : at + part.shape[0], :] = part
     side = BLOCK // 2
     zeros = jnp.zeros((2, 4 * rows, side), jnp.bfloat16)
     split[:, :, 0:side] = zeros
     split[:, :, side + columns : 2 * side + columns] = zeros
-    for copy in copies:
-        copy.wait()
 
     for k in range(reach + 1):
         block = edges[k].astype(jnp.float32)
@@ -259,10 +257,18 @@
                         split[0, q * rows + r : q * rows + r + 16, at : at + LANES] = high
                         split[1, q * rows + r : q * rows + r + 16, at : at + LANES] = low
             matrix = bands[half - HALVES[0]]
+            lane = lax.broadcasted_iota(jnp.int32, (4 * rows, LANES), 1)
             for c in range(0, columns, BLOCK):
-                window = jnp.concatenate(
-                    [split[0, :, c : c + 2 * BLOCK], split[1, :, c : c + 2 * BLOCK]], axis=1
-                )
+                middle = [split[n, :, side + c : side + c + BLOCK] for n in range(2)]
+                outer = [
+                    jnp.where(
+                        lane < LANES // 2,
+                        split[n, :, side + c + BLOCK : side + c + BLOCK + LANES],
+                        split[n, :, side + c - LANES : side + c],
+                    )
+                    for n in range(2)
+                ]
+                window = jnp.concatenate(middle + outer, axis=1)
                 box = jnp.dot(window, matrix, preferred_element_type=jnp.float32)
                 box_re, box_im, box_u, box_v = (box[q * rows : (q + 1) * rows] for q in range(4))
                 value = jnp.sqrt(box_re * box_re + box_im * box_im) * lax.rsqrt(box_u * box_v)
@@ -288,18 +294,14 @@
     return pl.pallas_call(
         functools.partial(coherence_kernel, reach, total_dates),
         out_shape=jax.ShapeDtypeStruct((dates, per_date, rows, columns), jnp.bfloat16),
-        in_specs=[pl.BlockSpec(memory_space=pltpu.HBM)] * 3 + [pl.BlockSpec(memory_space=pltpu.VMEM)] * 2,
+        in_specs=[pl.BlockSpec(memory_space=pltpu.SMEM)] * 3 + [pl.BlockSpec(memory_space=pltpu.VMEM)] * 2,
         out_specs=anywhere,
         scratch_shapes=[
             pltpu.VMEM((held, parts, 8, columns), jnp.float32),
             pltpu.VMEM((4, columns // LANES, rows + 16, LANES), jnp.float32),
-            pltpu.VMEM((len(HALVES), 4 * BLOCK, BLOCK), jnp.bfloat16),
+            pltpu.VMEM((len(HALVES), 3 * BLOCK, BLOCK), jnp.bfloat16),
             pltpu.VMEM((2, 4 * rows, columns + BLOCK), jnp.bfloat16),
             pltpu.VMEM((dates * per_date, rows, columns), jnp.bfloat16),
-            pltpu.SMEM(partners.shape, jnp.int32),
-            pltpu.SMEM(counts.shape, jnp.int32),
-            pltpu.SMEM(windows.shape, jnp.int32),
-            pltpu.SemaphoreType.DMA((3,)),
             pltpu.SemaphoreType.DMA((dates * per_date,)),
         ],
         compiler_params=pltpu.CompilerParams(vmem_limit_bytes=40 << 20),

time: 31.6 us -> 31.3 us (level)
  the two profiles are of different devices: /device:TPU:28 before, /device:TPU:26 now
where the time goes in v5:
time: 31.3 us; the launch traced here: 31 us
  Pallas kernels  27.9 us (89%)
  local copies, waits for them, and re-layouts  3.05 us (10%)
    pallas_call x1, Pallas kernels, exchange(): pl.pallas_call(functools.partial(exchange_kernel, loop_size, reach), out_...  20.8 us
    pallas_call x1, Pallas kernels, coherence(): pl.pallas_call(functools.partial(coherence_kernel, reach, total_dates), o...  7.09 us
    unnamed x8, local copies, waits for them, and re-layouts  3.05 us

profile of v5, /device:TPU:26, one launch (start us, length us, event | category | flops | bytes accessed | tf_op | source)
XLA Modules:
  0.0 31.0 jit_solution(15927698387246837214)
XLA Ops:
  0.0 0.0 copy-start
  0.0 1.0 %copy-done = bf16[2,2,64,1024]{3,2,1,0:T(8,128)(2,1)S(1)} copy-done((bf16[2,2,64,1024]{3,2,1,0:T(8,128)(2,1)S(1)}, bf16[2,2,64,1024]{3,2,1,0:T(8,128)(2,1)}, u32[]{:S(2)}) %copy-start) | copy-done | bytes 524312
  1.0 20.8 %exchange.1 = (bf16[3,2,2,64,1024]{4,3,2,1,0:T(8,128)(2,1)S(1)}, bf16[3,16,1024]{2,1,0:T(8,128)(2,1)S(1)}) custom-call(bf16[2,2,64,1024]{3,2,1,0:T(8,128)(2,1)S(1)} %copy-done), custom_call_target="tpu_custom_call" | custom-call | tf_op jit(solution)/shard_map/exchange/pallas_call | solution.py:144
  21.9 0.0 copy-start.1
  21.9 0.7 %copy-done.1 = s32[2,4]{1,0:T(2,128)S(1)} copy-done((s32[2,4]{1,0:T(2,128)S(1)}, s32[2,4]{1,0:T(2,128)}, u32[]{:S(2)}) %copy-start.1) | copy-done | bytes 56
  22.5 0.0 copy-start.2
  22.5 0.7 %copy-done.2 = s32[2,4]{1,0:T(2,128)S(1)} copy-done((s32[2,4]{1,0:T(2,128)S(1)}, s32[2,4]{1,0:T(2,128)}, u32[]{:S(2)}) %copy-start.2) | copy-done | bytes 56
  23.2 0.0 copy-start.3
  23.2 0.7 %copy-done.3 = s32[2]{0:T(128)S(1)} copy-done((s32[2]{0:T(128)S(1)}, s32[2]{0:T(128)}, u32[]{:S(2)}) %copy-start.3) | copy-done | bytes 32
  23.9 7.1 %coherence.1 = bf16[2,4,64,1024]{3,2,1,0:T(8,128)(2,1)} custom-call(s32[2,4]{1,0:T(2,128)S(1)} %copy-done.1, s32[2]{0:T(128)S(1)} %copy-done.3, s32[2,4]{1,0:T(2,128)S(1)} %copy-done.2, bf16[3,2,2,64,1024]{4,3,2,1,0:T(8,128)(2,1)S(1)} %get-tuple-element.7.held, bf16[3,16,1024]{2,1,0:T(8,128)(2,1)S(1)} %get-tuple-element.8.edges), custom_call_target="tpu_custom_call" | custom-call | tf_op jit(solution)/shard_map/coherence/pallas_call | solution.py:294
Async XLA Ops:
  0.0 1.0 %copy-start = (bf16[2,2,64,1024]{3,2,1,0:T(8,128)(2,1)S(1)}, bf16[2,2,64,1024]{3,2,1,0:T(8,128)(2,1)}, u32[]{:S(2)}) copy-start(bf16[2,2,64,1024]{3,2,1,0:T(8,128)(2,1)} %slc_ref.1) | copy-start | bytes 1572868
  21.9 0.7 %copy-start.1 = (s32[2,4]{1,0:T(2,128)S(1)}, s32[2,4]{1,0:T(2,128)}, u32[]{:S(2)}) copy-start(s32[2,4]{1,0:T(2,128)} %partner_ref.1) | copy-start | bytes 100
  22.5 0.7 %copy-start.2 = (s32[2,4]{1,0:T(2,128)S(1)}, s32[2,4]{1,0:T(2,128)}, u32[]{:S(2)}) copy-start(s32[2,4]{1,0:T(2,128)} %width_ref.1) | copy-start | bytes 100
  23.2 0.7 %copy-start.3 = (s32[2]{0:T(128)S(1)}, s32[2]{0:T(128)}, u32[]{:S(2)}) copy-start(s32[2]{0:T(128)} %count_ref.1) | copy-start | bytes 28
